TPU v7x, 128 devices: a whole 4x4x4 slice. The times are simulated.
128 devices in a mesh: tm: 16 (over y, z_lo, core), height: 8 (over z_hi, x).
Axes of the slice: x: 4, y: 4, z: 4 (z_hi: 2, z_lo: 2; z = z_hi * 2 + z_lo), core: 2. Of those that a mesh axis runs over, the one named last changes fastest.
Arguments:
- hidden: bfloat16 [32, 40, 80, 5120], P('tm', None, 'height'), may hold values from -256 to 256
- modulation: float32 [2, 4, 5120], replicated, may hold values from -3 to 3
- clip_lengths: int32 [4], replicated, may hold values from 1 to 10, 32 in all
- head_weight: bfloat16 [5120, 64], replicated, may hold values from -0.078125 to 0.078125
- head_bias: float32 [64], replicated, may hold values from -3 to 3
- conv_in_weight: bfloat16 [3, 3, 3, 16, 384], replicated, may hold values from -0.3125 to 0.3125
- conv_in_bias: float32 [384], replicated, may hold values from -3 to 3
- conv_out_weight: bfloat16 [3, 3, 3, 384, 384], replicated, may hold values from -0.0625 to 0.0625
- conv_out_bias: float32 [384], replicated, may hold values from -3 to 3
Outputs:
- decoded: bfloat16 [32, 80, 160, 384], P('tm', 'height')
Inputs may be any that keep to these rules, and one draw needn't show every extreme that they name: `clip_lengths`: clip lengths in frames; they sum to 32 and the longest is exactly 10.
All inputs are finite; a program needn't handle non-finite values.
Results may differ from a plain program's by a relative error of at most 0.0057.
Values may be sent and summed in bfloat16 or wider, within the bound.
A program may use at most 192 MiB of HBM per device.

v0:
```python
import functools

import jax
import jax.numpy as jnp
from jax import lax
from jax.experimental import pallas as pl
from jax.experimental.pallas import tpu as pltpu
from jax.sharding import PartitionSpec as P

F32 = jnp.float32
BF16 = jnp.bfloat16
MESH = pl.DeviceIdType.MESH


def clip_start(clip_ref, frame):
    first = jnp.int32(0)
    end = jnp.int32(0)
    for clip in range(clip_ref.shape[0] - 1):
        end = end + clip_ref[clip]
        first = jnp.where(frame >= end, end, first)
    return first


def conv_kernel(
    clip_ref, recv_ref, win_ref, bin_ref, wout_ref, bout_ref, out_ref,
    spread, tokens, dense_in, inner, raw, mixed, total, stage, packed, load_sem, store_sem,
    *, rows_per_step,
):
    slab = lax.axis_index("tm")
    band = lax.axis_index("height")
    frame0 = 2 * slab

    loads = []
    for part in range(9):
        cp = pltpu.make_async_copy(
            wout_ref.at[pl.ds(3 * part, 3)], raw.at[pl.ds(3 * part, 3)], load_sem.at[part]
        )
        cp.start()
        loads.append(cp)

    blank = jnp.zeros((16, 384), BF16)
    for a in range(3):
        for rr in range(4):
            for slot in range(4):
                for p in range(2):
                    for s in range(2):
                        b, e = rr - p, slot - s
                        ok = 0 <= b < 3 and 0 <= e < 3
                        row = a * 256 + rr * 64 + slot * 16
                        col = (2 * p + s) * 384
                        dense_in[row : row + 16, col : col + 384] = (
                            win_ref[9 * a + 3 * b + e] if ok else blank
                        )

    lane_in = lax.broadcasted_iota(jnp.int32, (128, 256), 0)
    lane_out = lax.broadcasted_iota(jnp.int32, (128, 256), 1)
    wanted = (
        (lane_out // 128) * 64
        + ((lane_out // 64) % 2) * 32
        + ((lane_out // 16 + 1) % 2) * 16
        + lane_out % 16
    )
    spreader = jnp.where(lane_in == wanted, 1.0, 0.0).astype(BF16)
    slot_id = (lax.broadcasted_iota(jnp.int32, (7, 10, 8, 128), 3) // 16) % 4
    group_id = lax.broadcasted_iota(jnp.int32, (7, 1, 8, 128), 2)
    for back in range(3):
        for src in range(8):
            block = recv_ref[back, src].astype(F32)
            for col in range(10):
                spread[back, pl.ds(8 * col + src, 8, stride=80), :] = block[8 * col : 8 * col + 8]
    for back in range(3):
        both = jnp.dot(spread[back, 0:560, :].astype(BF16), spreader, preferred_element_type=F32)
        for f in range(2):
            here = both[:, 128 * f : 128 * f + 128].reshape(7, 10, 8, 128)
            last = pltpu.roll(here[:, 9:10].reshape(56, 128), 1, 0).reshape(7, 1, 8, 128)
            last = jnp.where(group_id == 0, 0.0, last)
            head = pltpu.roll(here[:, 0:1].reshape(56, 128), 55, 0).reshape(7, 1, 8, 128)
            head = jnp.where(group_id == 7, 0.0, head)
            before = jnp.concatenate([last, here[:, 0:9]], axis=1)
            after = jnp.concatenate([here[:, 1:10], head], axis=1)
            mixed_slots = jnp.where(slot_id == 0, before, jnp.where(slot_id == 3, after, here))
            tokens[2 * back + f] = mixed_slots.reshape(560, 128).astype(BF16)

    keep = []
    for g in range(4):
        first = clip_start(clip_ref, frame0 - 2 + g)
        keep.append([frame0 - 4 + g + a >= first for a in range(3)])
    first0 = clip_start(clip_ref, frame0)
    use0 = frame0 - 2 >= first0
    use1 = frame0 - 1 >= first0
    joined = frame0 >= clip_start(clip_ref, frame0 + 1)
    c = jnp.where(joined, 1.0, 0.0).astype(F32)
    bias_in = bin_ref[...].reshape(1, 384)
    bias_in = jnp.concatenate([bias_in, bias_in], axis=1)

    def in_step(step, carry):
        i0 = 2 * step
        for p in range(2):
            x = []
            for g in range(4):
                parts = []
                for a in range(3):
                    lo = tokens[g + a, pl.ds(pl.multiple_of(i0 * 80, 16), 160), :]
                    hi = tokens[g + a, pl.ds(pl.multiple_of(i0 * 80 + 80, 16), 160), :]
                    both = jnp.concatenate([lo, hi], axis=1)
                    if a < 2:
                        both = jnp.where(keep[g][a], both, jnp.zeros_like(both))
                    parts.append(both)
                v = jnp.dot(
                    jnp.concatenate(parts, axis=1),
                    dense_in[:, 768 * p : 768 * p + 768],
                    preferred_element_type=F32,
                )
                v = 0.5 * (v + bias_in)
                v = v + v * jnp.tanh(v)
                x.append(v.astype(BF16).astype(F32))
            x0 = jnp.where(use0, x[0], 0.0)
            x1 = jnp.where(use1, x[1], 0.0)
            x2, x3 = x[2], x[3]
            sums = (x0 - c * x2, x1 + c * x2, x2 - c * x1, x3 - c * x1)
            for r in range(2):
                local = 4 * step + 2 * r + p
                h = 10 * band - 1 + local
                inside = jnp.logical_and(h >= 0, h < 80)
                for i in range(4):
                    part = sums[i][80 * r : 80 * r + 80]
                    inner[i, local] = jnp.where(inside, part, 0.0).astype(BF16)
        return carry

    lax.fori_loop(0, 3, in_step, 0)

    for cp in loads:
        cp.wait()

    def mix(k, carry):
        w0 = raw[k].astype(F32)
        w1 = raw[9 + k].astype(F32)
        w2 = raw[18 + k].astype(F32)
        outer = 0.5 * (w0 + w2)
        mid = 0.5 * w1
        mixed[0, k] = jnp.where(joined, outer + mid, w1).astype(BF16)
        mixed[1, k] = jnp.where(joined, outer - mid, w2).astype(BF16)
        return carry

    lax.fori_loop(0, 9, mix, 0)

    R = rows_per_step
    rows = 80 * R
    bias_out = bout_ref[...].reshape(1, 384)
    group_out = lax.broadcasted_iota(jnp.int32, (R, 1, 8, 384), 2)

    def weight(i, b, e):
        k = 3 * b + e
        if i == 0:
            return raw[k]
        if i == 3:
            return raw[18 + k]
        return mixed[i - 1, k]

    def product(i, h0):
        taps = [inner[i, pl.ds(h0 + b, R)].reshape(rows, 768) for b in range(3)]
        main_w = jnp.concatenate(
            [
                jnp.concatenate(
                    [
                        jnp.concatenate([weight(i, b, 1), weight(i, b, 0)], axis=1),
                        jnp.concatenate([weight(i, b, 2), weight(i, b, 1)], axis=1),
                    ],
                    axis=0,
                )
                for b in range(3)
            ],
            axis=0,
        )
        main = jnp.dot(jnp.concatenate(taps, axis=1), main_w, preferred_element_type=F32)
        left = jnp.dot(
            jnp.concatenate([tap[:, 384:] for tap in taps], axis=1),
            jnp.concatenate([weight(i, b, 0) for b in range(3)], axis=0),
            preferred_element_type=F32,
        )
        right = jnp.dot(
            jnp.concatenate([tap[:, :384] for tap in taps], axis=1),
            jnp.concatenate([weight(i, b, 2) for b in range(3)], axis=0),
            preferred_element_type=F32,
        )
        return (main, left, right)

    def finish(f, h0, main, left, right):
        left = left.reshape(R, 10, 8, 384)
        last = pltpu.roll(left[:, 9:10].reshape(8 * R, 384), 1, 0).reshape(R, 1, 8, 384)
        last = jnp.where(group_out == 0, 0.0, last)
        left = jnp.concatenate([last, left[:, 0:9]], axis=1).reshape(rows, 384)
        right = right.reshape(R, 10, 8, 384)
        head = pltpu.roll(right[:, 0:1].reshape(8 * R, 384), 8 * R - 1, 0).reshape(R, 1, 8, 384)
        head = jnp.where(group_out == 7, 0.0, head)
        right = jnp.concatenate([right[:, 1:10], head], axis=1).reshape(rows, 384)
        halves = (main[:, :384] + left + bias_out, main[:, 384:] + right + bias_out)
        for r in range(R):
            for s in range(2):
                for col in range(10):
                    at = 80 * r + 8 * col
                    for lane in range(3):
                        stage[f, 3 * r + lane, pl.ds(2 * col + s, 8, stride=20), :] = halves[s][
                            at : at + 8, 128 * lane : 128 * lane + 128
                        ]
        for r in range(R):
            for lane in range(3):
                packed[f, h0 + r, :, 128 * lane : 128 * lane + 128] = stage[
                    f, 3 * r + lane
                ].astype(BF16)

    def store(f, h0):
        return pltpu.make_async_copy(
            packed.at[f, pl.ds(h0, R)], out_ref.at[f, pl.ds(h0, R)], store_sem.at[f]
        )

    def out_step(step, carry):
        h0 = step * R
        m1 = product(1, h0)
        m2 = product(2, h0)
        at = (0, 768, 1152, 1536)
        for n, (u, v) in enumerate(zip(m1, m2)):
            total[0, :, at[n] : at[n + 1]] = u + v
            total[1, :, at[n] : at[n + 1]] = c * (u - v)
        for f in range(2):
            m = product(3 * f, h0)
            m = [total[f, :, at[n] : at[n + 1]] + u for n, u in enumerate(m)]
            finish(f, h0, *m)
            store(f, h0).start()
        return carry

    lax.fori_loop(0, 10 // R, out_step, 0)
    for f in range(2):
        pltpu.make_async_copy(packed.at[f], out_ref.at[f], store_sem.at[f]).wait()


def convolve(clip_lengths, received, conv_in_weight, conv_in_bias, conv_out_weight, conv_out_bias,
             rows_per_step=2):
    R = rows_per_step
    return pl.pallas_call(
        functools.partial(conv_kernel, rows_per_step=R),
        out_shape=jax.ShapeDtypeStruct((2, 10, 160, 384), BF16),
        in_specs=[
            pl.BlockSpec(memory_space=pltpu.SMEM),
            pl.BlockSpec(memory_space=pltpu.VMEM),
            pl.BlockSpec(memory_space=pltpu.VMEM),
            pl.BlockSpec(memory_space=pltpu.VMEM),
            pl.BlockSpec(memory_space=pl.ANY),
            pl.BlockSpec(memory_space=pltpu.VMEM),
        ],
        out_specs=pl.BlockSpec(memory_space=pl.ANY),
        scratch_shapes=[
            pltpu.VMEM((3, 640, 128), F32),
            pltpu.VMEM((6, 560, 128), BF16),
            pltpu.VMEM((768, 1536), BF16),
            pltpu.VMEM((4, 12, 80, 768), BF16),
            pltpu.VMEM((27, 384, 384), BF16),
            pltpu.VMEM((2, 9, 384, 384), BF16),
            pltpu.VMEM((2, 80 * R, 1536), F32),
            pltpu.VMEM((2, 3 * R, 160, 128), F32),
            pltpu.VMEM((2, 10, 160, 384), BF16),
            pltpu.SemaphoreType.DMA((9,)),
            pltpu.SemaphoreType.DMA((2,)),
        ],
        compiler_params=pltpu.CompilerParams(vmem_limit_bytes=60 << 20),
    )(
        clip_lengths,
        received,
        conv_in_weight.reshape(27, 16, 384),
        conv_in_bias,
        conv_out_weight.reshape(27, 384, 384),
        conv_out_bias,
    )


def head_kernel(
    clip_ref, hidden_ref, mod_ref, weight_ref, bias_ref, recv_ref,
    tokens, rhs, aux, raw, grid, outgoing, load_sem, send_sem, recv_sem,
):
    slab = lax.axis_index("tm")
    band = lax.axis_index("height")
    slabs = lax.axis_size("tm")
    bands = lax.axis_size("height")

    barrier = pltpu.get_barrier_semaphore()
    for d in range(3):
        for o in range(bands):
            if d or o:
                source = (lax.rem(slab + slabs - d, slabs), lax.rem(band + bands - o, bands))
                pl.semaphore_signal(barrier, inc=1, device_id=source, device_id_type=MESH)

    def load(n):
        return pltpu.make_async_copy(
            hidden_ref.at[pl.ds(pl.multiple_of(160 * n, 16), 160)], tokens.at[n], load_sem.at[n]
        )

    for n in range(5):
        load(n).start()

    weight = weight_ref[...].astype(F32)
    row_id = lax.broadcasted_iota(jnp.int32, (16, 5120), 0)
    extra = jnp.where(row_id == 0, 1.0, 0.0)
    for f in range(2):
        frame = 2 * slab + f
        end = jnp.int32(0)
        shift, scale = mod_ref[0, 0:1, :], mod_ref[1, 0:1, :]
        for clip in range(1, clip_ref.shape[0]):
            end = end + clip_ref[clip - 1]
            later = frame >= end
            shift = jnp.where(later, mod_ref[0, clip : clip + 1, :], shift)
            scale = jnp.where(later, mod_ref[1, clip : clip + 1, :], scale)
        rhs[64 * f : 64 * f + 64, :] = (weight * (1.0 + scale)).astype(BF16)
        rhs[128 + 64 * f : 192 + 64 * f, :] = weight_ref[...]
        coarse = shift.astype(BF16).astype(F32)
        extra = jnp.where(row_id == 2 * f + 1, coarse, extra)
        extra = jnp.where(row_id == 2 * f + 2, shift - coarse, extra)
    aux[...] = extra.astype(BF16)
    contract = (((1,), (1,)), ((), ()))
    sums = lax.dot_general(aux[...], rhs[...], contract, preferred_element_type=F32)
    lane = lax.broadcasted_iota(jnp.int32, (1, 128), 1)
    head_bias = bias_ref[...].reshape(1, 64)
    col_sum = sums[0:1, 0:128]
    offset = (
        jnp.where(lane < 64, sums[1:2, 128:] + sums[2:3, 128:], sums[3:4, 128:] + sums[4:5, 128:])
        + jnp.concatenate([head_bias, head_bias], axis=1)
    )

    zeros = jnp.zeros((8, 128), F32)
    for q in range(20):
        grid[56 * q : 56 * q + 8, :] = zeros
        grid[56 * q + 48 : 56 * q + 56, :] = zeros

    def head_step(n, carry):
        load(n).wait()
        raw[...] = lax.dot_general(
            tokens[n], rhs[0:128, :], contract, preferred_element_type=F32
        )

        def strip_step(k, inner_carry):
            at = pl.ds(pl.multiple_of(16 * k, 16), 16)
            pivot = jnp.sum(tokens[n, at, 0:128].astype(F32), axis=1, keepdims=True) / 128.0
            first = jnp.zeros((16, 128), F32)
            second = jnp.zeros((16, 128), F32)
            for tile in range(40):
                v = tokens[n, at, 128 * tile : 128 * tile + 128].astype(F32) - pivot
                first = first + v
                second = second + v * v
            first = jnp.sum(first, axis=1, keepdims=True) / 5120.0
            second = jnp.sum(second, axis=1, keepdims=True) / 5120.0
            scale = lax.rsqrt(second - first * first + 1e-06)
            value = scale * (raw[at, :] - (pivot + first) * col_sum) + offset
            for half in range(2):
                m = 20 * n + 2 * k + half
                row = (m // 5) * 56 + 8 + (m % 5) * 8
                grid[pl.ds(pl.multiple_of(row, 8), 8), :] = value[8 * half : 8 * half + 8]
            return inner_carry

        return lax.fori_loop(0, 10, strip_step, carry)

    lax.fori_loop(0, 5, head_step, 0)

    lane8 = lax.broadcasted_iota(jnp.int32, (8, 128), 1)
    for j in range(8):
        for pair in range(5):
            pieces = []
            for q in (2 * pair, 2 * pair + 1):
                at = 56 * q + 7 + 5 * j
                pieces.append(
                    jnp.where(lane8 < 64, grid[at : at + 8, :], grid[560 + at : 568 + at, :])
                )
            outgoing[j, 16 * pair : 16 * pair + 16, :] = jnp.concatenate(pieces, axis=0).astype(
                BF16
            )

    pl.semaphore_wait(barrier, 3 * bands - 1)
    copies = []
    for o in range(bands):
        to = lax.rem(band + o, bands)
        for d in range(3):
            target = recv_ref.at[2 - d, band]
            if d or o:
                cp = pltpu.make_async_remote_copy(
                    src_ref=outgoing.at[to],
                    dst_ref=target,
                    send_sem=send_sem.at[d, o],
                    recv_sem=recv_sem.at[d, o],
                    device_id=(lax.rem(slab + d, slabs), to),
                    device_id_type=MESH,
                )
            else:
                cp = pltpu.make_async_copy(outgoing.at[to], target, send_sem.at[d, o])
            cp.start()
            copies.append(cp)
    for cp in copies:
        cp.wait()


def head(clip_lengths, hidden, modulation, head_weight, head_bias):
    return pl.pallas_call(
        head_kernel,
        out_shape=jax.ShapeDtypeStruct((3, 8, 80, 128), BF16),
        in_specs=[
            pl.BlockSpec(memory_space=pltpu.SMEM),
            pl.BlockSpec(memory_space=pl.ANY),
            pl.BlockSpec(memory_space=pltpu.VMEM),
            pl.BlockSpec(memory_space=pltpu.VMEM),
            pl.BlockSpec(memory_space=pltpu.VMEM),
        ],
        out_specs=pl.BlockSpec(memory_space=pl.ANY),
        scratch_shapes=[
            pltpu.VMEM((5, 160, 5120), BF16),
            pltpu.VMEM((256, 5120), BF16),
            pltpu.VMEM((16, 5120), BF16),
            pltpu.VMEM((160, 128), F32),
            pltpu.VMEM((1120, 128), F32),
            pltpu.VMEM((8, 80, 128), BF16),
            pltpu.SemaphoreType.DMA((5,)),
            pltpu.SemaphoreType.DMA((3, 8)),
            pltpu.SemaphoreType.DMA((3, 8)),
        ],
        compiler_params=pltpu.CompilerParams(
            collective_id=0, has_side_effects=True, vmem_limit_bytes=60 << 20
        ),
    )(
        clip_lengths,
        hidden.transpose(0, 2, 1, 3).reshape(800, 5120),
        modulation,
        head_weight.T,
        head_bias,
    )


def on_device(
    hidden, modulation, clip_lengths, head_weight, head_bias,
    conv_in_weight, conv_in_bias, conv_out_weight, conv_out_bias,
):
    received = head(clip_lengths, hidden, modulation, head_weight, head_bias)
    return convolve(
        clip_lengths, received, conv_in_weight, conv_in_bias, conv_out_weight, conv_out_bias
    )


def solution(mesh):
    return jax.shard_map(
        on_device,
        mesh=mesh,
        in_specs=(P("tm", None, "height", None), P(), P(), P(), P(), P(), P(), P(), P()),
        out_specs=P("tm", "height", None, None),
        check_vma=False,
    )
```

profile of v0, /device:TPU:0, one launch (start us, length us, event | category | flops | bytes accessed | tf_op | source)
XLA Modules:
  0.0 65.1 jit_solution(8617507238791057305)
XLA Ops:
  0.0 30.7 %shard_map.91.recv_ref = bf16[3,8,80,128]{3,2,1,0:T(8,128)(2,1)} custom-call(s32[4]{0:T(128)} %clip_ref.3, bf16[800,5120]{1,0:T(8,128)(2,1)} %bitcast.6, f32[2,4,5120]{2,1,0:T(4,128)} %mod_ref.1, bf16[64,5120]{1,0:T(8,128)(2,1)} %bitcast.8, f32[64]{0:T(128)} %bias_ref.1), custom_call_target="tpu_custom_call" | custom-call | tf_op jit(solution)/shard_map/pallas_call | solution.py:399
  30.7 34.4 %shard_map.92 = bf16[2,10,160,384]{3,2,1,0:T(8,128)(2,1)} custom-call(s32[4]{0:T(128)} %clip_ref.3, bf16[3,8,80,128]{3,2,1,0:T(8,128)(2,1)} %shard_map.91.recv_ref, bf16[27,16,384]{2,1,0:T(8,128)(2,1)} %bitcast.9, f32[384]{0:T(512)} %bin_ref.1, bf16[27,384,384]{2,1,0:T(8,128)(2,1)} %bitcast.7, f32[384]{0:T(512)} %bout_ref.1), custom_call_target="tpu_custom_call" | custom-call | tf_op jit(solution)/shard_map/pallas_call | solution.py:240
where the time goes:
time: 65.3 us; the launch traced here: 65.1 us
  Pallas kernels  65.1 us (100%)
    pallas_call x1, Pallas kernels, convolve(): pl.pallas_call(functools.partial(conv_kernel, rows_per_step=R), out_shape...  34.4 us
    pallas_call x1, Pallas kernels, head(): pl.pallas_call(head_kernel, out_shape=jax.ShapeDtypeStruct((3, 8, 80, 128...  30.7 us

commit v1 on v0

--- a/solution.py
+++ b/solution.py
@@ -22,35 +22,24 @@
 
 
 def conv_kernel(
-    clip_ref, recv_ref, win_ref, bin_ref, wout_ref, bout_ref, out_ref,
-    spread, tokens, dense_in, inner, raw, mixed, total, stage, packed, load_sem, store_sem,
-    *, rows_per_step,
+    clip_ref, recv_ref, dense_ref, bin_ref, wout_ref, mixed_ref, bout_ref, out_ref,
+    received, spread, tokens, dense_in, inner, weights, total, stage, packed,
+    recv_sem, load_sem, store_sem, *, rows_per_step,
 ):
     slab = lax.axis_index("tm")
     band = lax.axis_index("height")
     frame0 = 2 * slab
 
-    loads = []
-    for part in range(9):
-        cp = pltpu.make_async_copy(
-            wout_ref.at[pl.ds(3 * part, 3)], raw.at[pl.ds(3 * part, 3)], load_sem.at[part]
-        )
-        cp.start()
-        loads.append(cp)
-
-    blank = jnp.zeros((16, 384), BF16)
-    for a in range(3):
-        for rr in range(4):
-            for slot in range(4):
-                for p in range(2):
-                    for s in range(2):
-                        b, e = rr - p, slot - s
-                        ok = 0 <= b < 3 and 0 <= e < 3
-                        row = a * 256 + rr * 64 + slot * 16
-                        col = (2 * p + s) * 384
-                        dense_in[row : row + 16, col : col + 384] = (
-                            win_ref[9 * a + 3 * b + e] if ok else blank
-                        )
+    recv_copy = pltpu.make_async_copy(recv_ref, received, recv_sem)
+    recv_copy.start()
+    dense_copy = pltpu.make_async_copy(dense_ref, dense_in, load_sem.at[4])
+    dense_copy.start()
+    sources = (
+        wout_ref.at[pl.ds(0, 9)], mixed_ref.at[0], mixed_ref.at[1], wout_ref.at[pl.ds(18, 9)]
+    )
+    loads = [
+        pltpu.make_async_copy(sources[i], weights.at[i], load_sem.at[i]) for i in range(4)
+    ]
 
     lane_in = lax.broadcasted_iota(jnp.int32, (128, 256), 0)
     lane_out = lax.broadcasted_iota(jnp.int32, (128, 256), 1)
@@ -63,9 +52,10 @@
     spreader = jnp.where(lane_in == wanted, 1.0, 0.0).astype(BF16)
     slot_id = (lax.broadcasted_iota(jnp.int32, (7, 10, 8, 128), 3) // 16) % 4
     group_id = lax.broadcasted_iota(jnp.int32, (7, 1, 8, 128), 2)
+    recv_copy.wait()
     for back in range(3):
         for src in range(8):
-            block = recv_ref[back, src].astype(F32)
+            block = received[back, src].astype(F32)
             for col in range(10):
                 spread[back, pl.ds(8 * col + src, 8, stride=80), :] = block[8 * col : 8 * col + 8]
     for back in range(3):
@@ -90,8 +80,12 @@
     use1 = frame0 - 1 >= first0
     joined = frame0 >= clip_start(clip_ref, frame0 + 1)
     c = jnp.where(joined, 1.0, 0.0).astype(F32)
-    bias_in = bin_ref[...].reshape(1, 384)
+    c16 = c.astype(BF16)
+    bias_in = 0.5 * bin_ref[...].reshape(1, 384)
     bias_in = jnp.concatenate([bias_in, bias_in], axis=1)
+    dense_copy.wait()
+    for i in (1, 2, 0, 3):
+        loads[i].start()
 
     def in_step(step, carry):
         i0 = 2 * step
@@ -111,38 +105,31 @@
                     dense_in[:, 768 * p : 768 * p + 768],
                     preferred_element_type=F32,
                 )
-                v = 0.5 * (v + bias_in)
-                v = v + v * jnp.tanh(v)
-                x.append(v.astype(BF16).astype(F32))
-            x0 = jnp.where(use0, x[0], 0.0)
-            x1 = jnp.where(use1, x[1], 0.0)
+                v = v + bias_in
+                x.append((v + v * jnp.tanh(v)).astype(BF16))
+            zero = jnp.zeros_like(x[0])
+            x0 = jnp.where(use0, x[0], zero)
+            x1 = jnp.where(use1, x[1], zero)
             x2, x3 = x[2], x[3]
-            sums = (x0 - c * x2, x1 + c * x2, x2 - c * x1, x3 - c * x1)
+            x1c, x2c = c16 * x1, c16 * x2
+            sums = (x0 - x2c, x1 + x2c, x2 - x1c, x3 - x1c)
             for r in range(2):
-                local = 4 * step + 2 * r + p
-                h = 10 * band - 1 + local
-                inside = jnp.logical_and(h >= 0, h < 80)
                 for i in range(4):
-                    part = sums[i][80 * r : 80 * r + 80]
-                    inner[i, local] = jnp.where(inside, part, 0.0).astype(BF16)
+                    inner[i, 4 * step + 2 * r + p] = sums[i][80 * r : 80 * r + 80]
         return carry
 
     lax.fori_loop(0, 3, in_step, 0)
+
+    @pl.when(band == 0)
+    def _():
+        inner[:, 0] = jnp.zeros((4, 80, 768), BF16)
+
+    @pl.when(band == 7)
+    def _():
+        inner[:, 11] = jnp.zeros((4, 80, 768), BF16)
 
     for cp in loads:
         cp.wait()
-
-    def mix(k, carry):
-        w0 = raw[k].astype(F32)
-        w1 = raw[9 + k].astype(F32)
-        w2 = raw[18 + k].astype(F32)
-        outer = 0.5 * (w0 + w2)
-        mid = 0.5 * w1
-        mixed[0, k] = jnp.where(joined, outer + mid, w1).astype(BF16)
-        mixed[1, k] = jnp.where(joined, outer - mid, w2).astype(BF16)
-        return carry
-
-    lax.fori_loop(0, 9, mix, 0)
 
     R = rows_per_step
     rows = 80 * R
@@ -150,12 +137,7 @@
     group_out = lax.broadcasted_iota(jnp.int32, (R, 1, 8, 384), 2)
 
     def weight(i, b, e):
-        k = 3 * b + e
-        if i == 0:
-            return raw[k]
-        if i == 3:
-            return raw[18 + k]
-        return mixed[i - 1, k]
+        return weights[i, 3 * b + e]
 
     def product(i, h0):
         taps = [inner[i, pl.ds(h0 + b, R)].reshape(rows, 768) for b in range(3)]
@@ -214,68 +196,83 @@
             packed.at[f, pl.ds(h0, R)], out_ref.at[f, pl.ds(h0, R)], store_sem.at[f]
         )
 
+    at = (0, 768, 1152, 1536)
+
+    def finish_both(h0):
+        for f in range(2):
+            finish(f, h0, *[total[f, :, at[n] : at[n + 1]] for n in range(3)])
+
     def out_step(step, carry):
         h0 = step * R
+        finish_both(jnp.maximum(h0 - R, 0))
         m1 = product(1, h0)
         m2 = product(2, h0)
-        at = (0, 768, 1152, 1536)
-        for n, (u, v) in enumerate(zip(m1, m2)):
-            total[0, :, at[n] : at[n + 1]] = u + v
-            total[1, :, at[n] : at[n + 1]] = c * (u - v)
-        for f in range(2):
-            m = product(3 * f, h0)
-            m = [total[f, :, at[n] : at[n + 1]] + u for n, u in enumerate(m)]
-            finish(f, h0, *m)
-            store(f, h0).start()
+        m0 = product(0, h0)
+        for n, (u, v, w) in enumerate(zip(m0, m1, m2)):
+            total[0, :, at[n] : at[n + 1]] = u + (v + w)
+            total[1, :, at[n] : at[n + 1]] = c * (v - w)
+        for n, u in enumerate(product(3, h0)):
+            total[1, :, at[n] : at[n + 1]] = total[1, :, at[n] : at[n + 1]] + u
+
+        @pl.when(step > 0)
+        def _():
+            store(0, h0 - R).start()
+            store(1, h0 - R).start()
+
         return carry
 
     lax.fori_loop(0, 10 // R, out_step, 0)
+    finish_both(10 - R)
+    for f in range(2):
+        store(f, 10 - R).start()
     for f in range(2):
         pltpu.make_async_copy(packed.at[f], out_ref.at[f], store_sem.at[f]).wait()
 
 
-def convolve(clip_lengths, received, conv_in_weight, conv_in_bias, conv_out_weight, conv_out_bias,
-             rows_per_step=2):
+def convolve(
+    clip_lengths, received, dense_in, conv_in_bias, conv_out_weight, mixed, conv_out_bias,
+    rows_per_step=5,
+):
     R = rows_per_step
     return pl.pallas_call(
         functools.partial(conv_kernel, rows_per_step=R),
         out_shape=jax.ShapeDtypeStruct((2, 10, 160, 384), BF16),
         in_specs=[
             pl.BlockSpec(memory_space=pltpu.SMEM),
+            pl.BlockSpec(memory_space=pl.ANY),
+            pl.BlockSpec(memory_space=pl.ANY),
             pl.BlockSpec(memory_space=pltpu.VMEM),
-            pl.BlockSpec(memory_space=pltpu.VMEM),
-            pl.BlockSpec(memory_space=pltpu.VMEM),
+            pl.BlockSpec(memory_space=pl.ANY),
             pl.BlockSpec(memory_space=pl.ANY),
             pl.BlockSpec(memory_space=pltpu.VMEM),
         ],
         out_specs=pl.BlockSpec(memory_space=pl.ANY),
         scratch_shapes=[
+            pltpu.VMEM((3, 8, 80, 128), BF16),
             pltpu.VMEM((3, 640, 128), F32),
             pltpu.VMEM((6, 560, 128), BF16),
             pltpu.VMEM((768, 1536), BF16),
             pltpu.VMEM((4, 12, 80, 768), BF16),
-            pltpu.VMEM((27, 384, 384), BF16),
-            pltpu.VMEM((2, 9, 384, 384), BF16),
+            pltpu.VMEM((4, 9, 384, 384), BF16),
             pltpu.VMEM((2, 80 * R, 1536), F32),
             pltpu.VMEM((2, 3 * R, 160, 128), F32),
             pltpu.VMEM((2, 10, 160, 384), BF16),
-            pltpu.SemaphoreType.DMA((9,)),
+            pltpu.SemaphoreType.DMA,
+            pltpu.SemaphoreType.DMA((5,)),
             pltpu.SemaphoreType.DMA((2,)),
         ],
         compiler_params=pltpu.CompilerParams(vmem_limit_bytes=60 << 20),
     )(
-        clip_lengths,
-        received,
-        conv_in_weight.reshape(27, 16, 384),
-        conv_in_bias,
-        conv_out_weight.reshape(27, 384, 384),
-        conv_out_bias,
+        clip_lengths, received, dense_in, conv_in_bias,
+        conv_out_weight.reshape(27, 384, 384), mixed, conv_out_bias,
     )
 
 
 def head_kernel(
-    clip_ref, hidden_ref, mod_ref, weight_ref, bias_ref, recv_ref,
-    tokens, rhs, aux, raw, grid, outgoing, load_sem, send_sem, recv_sem,
+    clip_ref, hidden_ref, mod_ref, weight_ref, bias_ref, win_ref, wout_ref,
+    recv_ref, dense_ref, mixed_ref,
+    tokens, rhs, aux, grid, outgoing, win, dense_in, raw, mixed,
+    load_sem, weight_sem, store_sem, send_sem, recv_sem,
 ):
     slab = lax.axis_index("tm")
     band = lax.axis_index("height")
@@ -296,6 +293,14 @@
 
     for n in range(5):
         load(n).start()
+    win_copy = pltpu.make_async_copy(win_ref, win, weight_sem.at[3])
+    win_copy.start()
+    raw_copies = [
+        pltpu.make_async_copy(wout_ref.at[pl.ds(9 * a, 9)], raw.at[a], weight_sem.at[a])
+        for a in range(3)
+    ]
+    for cp in raw_copies:
+        cp.start()
 
     weight = weight_ref[...].astype(F32)
     row_id = lax.broadcasted_iota(jnp.int32, (16, 5120), 0)
@@ -332,30 +337,32 @@
 
     def head_step(n, carry):
         load(n).wait()
-        raw[...] = lax.dot_general(
-            tokens[n], rhs[0:128, :], contract, preferred_element_type=F32
-        )
-
-        def strip_step(k, inner_carry):
-            at = pl.ds(pl.multiple_of(16 * k, 16), 16)
-            pivot = jnp.sum(tokens[n, at, 0:128].astype(F32), axis=1, keepdims=True) / 128.0
+        raw = lax.dot_general(tokens[n], rhs[0:128, :], contract, preferred_element_type=F32)
+        pivots, firsts, seconds = [], [], []
+        for k in range(10):
+            at = slice(16 * k, 16 * k + 16)
+            pivot = tokens[n, at, 0:128].astype(F32)
             first = jnp.zeros((16, 128), F32)
             second = jnp.zeros((16, 128), F32)
-            for tile in range(40):
+            for tile in range(1, 40):
                 v = tokens[n, at, 128 * tile : 128 * tile + 128].astype(F32) - pivot
                 first = first + v
                 second = second + v * v
-            first = jnp.sum(first, axis=1, keepdims=True) / 5120.0
-            second = jnp.sum(second, axis=1, keepdims=True) / 5120.0
-            scale = lax.rsqrt(second - first * first + 1e-06)
-            value = scale * (raw[at, :] - (pivot + first) * col_sum) + offset
-            for half in range(2):
-                m = 20 * n + 2 * k + half
-                row = (m // 5) * 56 + 8 + (m % 5) * 8
-                grid[pl.ds(pl.multiple_of(row, 8), 8), :] = value[8 * half : 8 * half + 8]
-            return inner_carry
-
-        return lax.fori_loop(0, 10, strip_step, carry)
+            pivots.append(pivot)
+            firsts.append(first)
+            seconds.append(second)
+        pivot = jnp.concatenate(pivots, axis=0)
+        first = jnp.concatenate(firsts, axis=0)
+        second = jnp.concatenate(seconds, axis=0)
+        mean = jnp.sum(40.0 * pivot + first, axis=1, keepdims=True) / 5120.0
+        gap = mean - pivot
+        spread = second - 2.0 * gap * first + 40.0 * gap * gap
+        scale = lax.rsqrt(jnp.sum(spread, axis=1, keepdims=True) / 5120.0 + 1e-06)
+        value = scale * (raw - mean * col_sum) + offset
+        for m in range(20):
+            row = (4 * n + m // 5) * 56 + 8 + (m % 5) * 8
+            grid[pl.ds(pl.multiple_of(row, 8), 8), :] = value[8 * m : 8 * m + 8]
+        return carry
 
     lax.fori_loop(0, 5, head_step, 0)
 
@@ -391,30 +398,85 @@
                 cp = pltpu.make_async_copy(outgoing.at[to], target, send_sem.at[d, o])
             cp.start()
             copies.append(cp)
-    for cp in copies:
+
+    win_copy.wait()
+    blank = jnp.zeros((16, 384), BF16)
+    half = jnp.asarray(0.5, BF16)
+    for a in range(3):
+        for rr in range(4):
+            for slot in range(4):
+                for p in range(2):
+                    for s in range(2):
+                        b, e = rr - p, slot - s
+                        ok = 0 <= b < 3 and 0 <= e < 3
+                        row = a * 256 + rr * 64 + slot * 16
+                        col = (2 * p + s) * 384
+                        dense_in[row : row + 16, col : col + 384] = (
+                            win[9 * a + 3 * b + e] * half if ok else blank
+                        )
+    dense_store = pltpu.make_async_copy(dense_in, dense_ref, store_sem.at[2])
+    dense_store.start()
+
+    second = 2 * slab + 1
+    starts = second == 0
+    end = jnp.int32(0)
+    for clip in range(clip_ref.shape[0] - 1):
+        end = end + clip_ref[clip]
+        starts = jnp.logical_or(starts, second == end)
+    for cp in raw_copies:
         cp.wait()
 
-
-def head(clip_lengths, hidden, modulation, head_weight, head_bias):
+    def mix(k, carry):
+        w0, w1, w2 = (raw[a, k].astype(F32) for a in range(3))
+        outer = 0.5 * (w0 + w2)
+        mid = 0.5 * w1
+        mixed[0, k] = jnp.where(starts, w1, outer + mid).astype(BF16)
+        mixed[1, k] = jnp.where(starts, w2, outer - mid).astype(BF16)
+        return carry
+
+    lax.fori_loop(0, 9, mix, 0)
+    mixed_stores = [
+        pltpu.make_async_copy(mixed.at[i], mixed_ref.at[i], store_sem.at[i]) for i in range(2)
+    ]
+    for cp in mixed_stores:
+        cp.start()
+    for cp in copies + mixed_stores + [dense_store]:
+        cp.wait()
+
+
+def head(
+    clip_lengths, hidden, modulation, head_weight, head_bias, conv_in_weight, conv_out_weight
+):
     return pl.pallas_call(
         head_kernel,
-        out_shape=jax.ShapeDtypeStruct((3, 8, 80, 128), BF16),
+        out_shape=(
+            jax.ShapeDtypeStruct((3, 8, 80, 128), BF16),
+            jax.ShapeDtypeStruct((768, 1536), BF16),
+            jax.ShapeDtypeStruct((2, 9, 384, 384), BF16),
+        ),
         in_specs=[
             pl.BlockSpec(memory_space=pltpu.SMEM),
             pl.BlockSpec(memory_space=pl.ANY),
             pl.BlockSpec(memory_space=pltpu.VMEM),
             pl.BlockSpec(memory_space=pltpu.VMEM),
             pl.BlockSpec(memory_space=pltpu.VMEM),
+            pl.BlockSpec(memory_space=pl.ANY),
+            pl.BlockSpec(memory_space=pl.ANY),
         ],
-        out_specs=pl.BlockSpec(memory_space=pl.ANY),
+        out_specs=[pl.BlockSpec(memory_space=pl.ANY)] * 3,
         scratch_shapes=[
             pltpu.VMEM((5, 160, 5120), BF16),
             pltpu.VMEM((256, 5120), BF16),
             pltpu.VMEM((16, 5120), BF16),
-            pltpu.VMEM((160, 128), F32),
             pltpu.VMEM((1120, 128), F32),
             pltpu.VMEM((8, 80, 128), BF16),
+            pltpu.VMEM((27, 16, 384), BF16),
+            pltpu.VMEM((768, 1536), BF16),
+            pltpu.VMEM((3, 9, 384, 384), BF16),
+            pltpu.VMEM((2, 9, 384, 384), BF16),
             pltpu.SemaphoreType.DMA((5,)),
+            pltpu.SemaphoreType.DMA((4,)),
+            pltpu.SemaphoreType.DMA((3,)),
             pltpu.SemaphoreType.DMA((3, 8)),
             pltpu.SemaphoreType.DMA((3, 8)),
         ],
@@ -427,6 +489,8 @@
         modulation,
         head_weight.T,
         head_bias,
+        conv_in_weight.reshape(27, 16, 384),
+        conv_out_weight.reshape(27, 384, 384),
     )
 
 
@@ -434,9 +498,11 @@
     hidden, modulation, clip_lengths, head_weight, head_bias,
     conv_in_weight, conv_in_bias, conv_out_weight, conv_out_bias,
 ):
-    received = head(clip_lengths, hidden, modulation, head_weight, head_bias)
+    received, dense_in, mixed = head(
+        clip_lengths, hidden, modulation, head_weight, head_bias, conv_in_weight, conv_out_weight
+    )
     return convolve(
-        clip_lengths, received, conv_in_weight, conv_in_bias, conv_out_weight, conv_out_bias
+        clip_lengths, received, dense_in, conv_in_bias, conv_out_weight, mixed, conv_out_bias
     )
 
 

time: 65.3 us -> 53.2 us (0.81)
  Pallas kernels: 65.1 us -> 52.9 us
    pallas_call x1, Pallas kernels: 30.7 us -> 21.6 us  [head(): pl.pallas_call(head_kernel, out_shape=(jax.ShapeDtypeStruct((3, 8, 80, 12...]
    pallas_call x1, Pallas kernels: 34.4 us -> 31.2 us  [convolve(): pl.pallas_call(functools.partial(conv_kernel, rows_per_step=R), out_shape...]
where the time goes in v1:
time: 53.2 us; the launch traced here: 53.1 us
  Pallas kernels  52.9 us (99%)
    pallas_call x1, Pallas kernels, convolve(): pl.pallas_call(functools.partial(conv_kernel, rows_per_step=R), out_shape...  31.2 us
    pallas_call x1, Pallas kernels, head(): pl.pallas_call(head_kernel, out_shape=(jax.ShapeDtypeStruct((3, 8, 80, 12...  21.6 us

profile of v1, /device:TPU:0, one launch (start us, length us, event | category | flops | bytes accessed | tf_op | source)
XLA Modules:
  0.0 53.1 jit_solution(15902764118421808289)
XLA Ops:
  0.0 21.6 %shard_map.91 = (bf16[3,8,80,128]{3,2,1,0:T(8,128)(2,1)}, bf16[768,1536]{1,0:T(8,128)(2,1)}, bf16[2,9,384,384]{3,2,1,0:T(8,128)(2,1)}) custom-call(s32[4]{0:T(128)} %clip_ref.3, bf16[800,5120]{1,0:T(8,128)(2,1)} %bitcast.8, f32[2,4,5120]{2,1,0:T(4,128)} %mod_ref.1, bf16[64,5120]{1,0:T(8,128)(2,1)} %bitcast.9, f32[64]{0:T(128)} %bias_ref.1, ...), custom_call_target="tpu_custom_call" | custom-call | tf_op jit(solution)/shard_map/pallas_call | solution.py:450
  21.7 31.2 %shard_map.92 = bf16[2,10,160,384]{3,2,1,0:T(8,128)(2,1)} custom-call(s32[4]{0:T(128)} %clip_ref.3, bf16[3,8,80,128]{3,2,1,0:T(8,128)(2,1)} %get-tuple-element.8.recv_ref, bf16[768,1536]{1,0:T(8,128)(2,1)} %get-tuple-element.9.dense_ref, f32[384]{0:T(512)} %bin_ref.1, bf16[27,384,384]{2,1,0:T(8,128)(2,1)} %bitcast.7, ...), custom_call_target="tpu_custom_call" | custom-call | tf_op jit(solution)/shard_map/pallas_call | solution.py:237

commit v2 on v1

--- a/solution.py
+++ b/solution.py
@@ -81,6 +81,8 @@
     joined = frame0 >= clip_start(clip_ref, frame0 + 1)
     c = jnp.where(joined, 1.0, 0.0).astype(F32)
     c16 = c.astype(BF16)
+    halved = jnp.where(joined, 0.5, 1.0).astype(F32)
+    paired = jnp.where(joined, 0.5, 0.0).astype(F32)
     bias_in = 0.5 * bin_ref[...].reshape(1, 384)
     bias_in = jnp.concatenate([bias_in, bias_in], axis=1)
     dense_copy.wait()
@@ -209,8 +211,8 @@
         m2 = product(2, h0)
         m0 = product(0, h0)
         for n, (u, v, w) in enumerate(zip(m0, m1, m2)):
-            total[0, :, at[n] : at[n + 1]] = u + (v + w)
-            total[1, :, at[n] : at[n + 1]] = c * (v - w)
+            total[0, :, at[n] : at[n + 1]] = u + halved * (v + w)
+            total[1, :, at[n] : at[n + 1]] = paired * (v - w)
         for n, u in enumerate(product(3, h0)):
             total[1, :, at[n] : at[n + 1]] = total[1, :, at[n] : at[n + 1]] + u
 
@@ -271,133 +273,156 @@
 def head_kernel(
     clip_ref, hidden_ref, mod_ref, weight_ref, bias_ref, win_ref, wout_ref,
     recv_ref, dense_ref, mixed_ref,
-    tokens, rhs, aux, grid, outgoing, win, dense_in, raw, mixed,
-    load_sem, weight_sem, store_sem, send_sem, recv_sem,
+    tokens, mod, weight, rhs, aux, raw, moments, grid, outgoing, win, dense_in, taps, mixed,
+    load_sem, small_sem, tap_sem, store_sem, send_sem, recv_sem,
 ):
     slab = lax.axis_index("tm")
     band = lax.axis_index("height")
     slabs = lax.axis_size("tm")
     bands = lax.axis_size("height")
-
-    barrier = pltpu.get_barrier_semaphore()
-    for d in range(3):
-        for o in range(bands):
-            if d or o:
-                source = (lax.rem(slab + slabs - d, slabs), lax.rem(band + bands - o, bands))
-                pl.semaphore_signal(barrier, inc=1, device_id=source, device_id_type=MESH)
+    small = [
+        pltpu.make_async_copy(weight_ref, weight, small_sem.at[0]),
+        pltpu.make_async_copy(mod_ref, mod, small_sem.at[1]),
+    ]
+    for cp in small:
+        cp.start()
 
     def load(n):
         return pltpu.make_async_copy(
             hidden_ref.at[pl.ds(pl.multiple_of(160 * n, 16), 160)], tokens.at[n], load_sem.at[n]
         )
 
-    for n in range(5):
+    for n in range(1):
         load(n).start()
-    win_copy = pltpu.make_async_copy(win_ref, win, weight_sem.at[3])
+    win_copy = pltpu.make_async_copy(win_ref, win, small_sem.at[2])
     win_copy.start()
-    raw_copies = [
-        pltpu.make_async_copy(wout_ref.at[pl.ds(9 * a, 9)], raw.at[a], weight_sem.at[a])
-        for a in range(3)
-    ]
-    for cp in raw_copies:
-        cp.start()
-
-    weight = weight_ref[...].astype(F32)
+
+    barrier = pltpu.get_barrier_semaphore()
+    for d in range(3):
+
+        @pl.when(slab >= d)
+        def _():
+            for o in range(bands):
+                if d or o:
+                    source = (slab - d, lax.rem(band + bands - o, bands))
+                    pl.semaphore_signal(barrier, inc=1, device_id=source, device_id_type=MESH)
+
+    def load_taps(k):
+        at = pl.ds(3 * k, 3)
+        return pltpu.make_async_copy(wout_ref.at[:, at], taps.at[:, at], tap_sem.at[k])
+
+    for cp in small:
+        cp.wait()
+    for n in range(1, 3):
+        load(n).start()
+    weights = weight[...].astype(F32)
     row_id = lax.broadcasted_iota(jnp.int32, (16, 5120), 0)
     extra = jnp.where(row_id == 0, 1.0, 0.0)
+    scaled = []
     for f in range(2):
         frame = 2 * slab + f
         end = jnp.int32(0)
-        shift, scale = mod_ref[0, 0:1, :], mod_ref[1, 0:1, :]
+        shift, scale = mod[0, 0:1, :], mod[1, 0:1, :]
         for clip in range(1, clip_ref.shape[0]):
             end = end + clip_ref[clip - 1]
             later = frame >= end
-            shift = jnp.where(later, mod_ref[0, clip : clip + 1, :], shift)
-            scale = jnp.where(later, mod_ref[1, clip : clip + 1, :], scale)
-        rhs[64 * f : 64 * f + 64, :] = (weight * (1.0 + scale)).astype(BF16)
-        rhs[128 + 64 * f : 192 + 64 * f, :] = weight_ref[...]
+            shift = jnp.where(later, mod[0, clip : clip + 1, :], shift)
+            scale = jnp.where(later, mod[1, clip : clip + 1, :], scale)
+        scaled.append((weights * (1.0 + scale)).astype(BF16))
         coarse = shift.astype(BF16).astype(F32)
         extra = jnp.where(row_id == 2 * f + 1, coarse, extra)
         extra = jnp.where(row_id == 2 * f + 2, shift - coarse, extra)
     aux[...] = extra.astype(BF16)
     contract = (((1,), (1,)), ((), ()))
-    sums = lax.dot_general(aux[...], rhs[...], contract, preferred_element_type=F32)
-    lane = lax.broadcasted_iota(jnp.int32, (1, 128), 1)
+    scaled = jnp.concatenate(scaled, axis=0)
+    ones = jnp.ones((128, 128), BF16)
+    for k in range(40):
+        rhs[128 * k : 128 * k + 128, 0:128] = scaled[:, 128 * k : 128 * k + 128].T
+        rhs[128 * k : 128 * k + 128, 128:256] = ones
+    col_sum = jnp.dot(aux[...], rhs[...], preferred_element_type=F32)[0:1, 0:128]
+    sums = lax.dot_general(aux[...], weight[...], contract, preferred_element_type=F32)
     head_bias = bias_ref[...].reshape(1, 64)
-    col_sum = sums[0:1, 0:128]
-    offset = (
-        jnp.where(lane < 64, sums[1:2, 128:] + sums[2:3, 128:], sums[3:4, 128:] + sums[4:5, 128:])
-        + jnp.concatenate([head_bias, head_bias], axis=1)
-    )
-
-    zeros = jnp.zeros((8, 128), F32)
-    for q in range(20):
-        grid[56 * q : 56 * q + 8, :] = zeros
-        grid[56 * q + 48 : 56 * q + 56, :] = zeros
+    offset = jnp.concatenate(
+        [sums[1:2] + sums[2:3] + head_bias, sums[3:4] + sums[4:5] + head_bias], axis=1
+    )
+
+    grid[...] = jnp.zeros_like(grid)
+    lane8 = lax.broadcasted_iota(jnp.int32, (8, 128), 1)
+
+    def settle(n):
+        pivot, second = moments[0], moments[1]
+        mean = raw[:, 128:256] * (1.0 / 5120.0)
+        gap = mean - pivot
+        var = jnp.sum(second, axis=1, keepdims=True) * (1.0 / 5120.0) - gap * gap
+        value = lax.rsqrt(var + 1e-06) * (raw[:, 0:128] - mean * col_sum) + offset
+        for m in range(20):
+            q = 4 * n + m // 5
+            own = (lane8 < 64) == (q < 10)
+            row = lax.rem(q, 10) * 56 + 8 + (m % 5) * 8
+            at = pl.ds(pl.multiple_of(row, 8), 8)
+            grid[at, :] = jnp.where(own, value[8 * m : 8 * m + 8], grid[at, :])
 
     def head_step(n, carry):
         load(n).wait()
-        raw = lax.dot_general(tokens[n], rhs[0:128, :], contract, preferred_element_type=F32)
-        pivots, firsts, seconds = [], [], []
+
+        @pl.when(n < 2)
+        def _():
+            load(n + 3).start()
+
+        settle(jnp.maximum(n - 1, 0))
+        sample = jnp.sum(tokens[n, :, 0:128].astype(F32), axis=1, keepdims=True) * (1.0 / 128.0)
+        pivot = jnp.broadcast_to(sample, (160, 128))
+        moments[0] = pivot
         for k in range(10):
             at = slice(16 * k, 16 * k + 16)
-            pivot = tokens[n, at, 0:128].astype(F32)
-            first = jnp.zeros((16, 128), F32)
             second = jnp.zeros((16, 128), F32)
-            for tile in range(1, 40):
-                v = tokens[n, at, 128 * tile : 128 * tile + 128].astype(F32) - pivot
-                first = first + v
+            for tile in range(40):
+                v = tokens[n, at, 128 * tile : 128 * tile + 128].astype(F32) - pivot[at]
                 second = second + v * v
-            pivots.append(pivot)
-            firsts.append(first)
-            seconds.append(second)
-        pivot = jnp.concatenate(pivots, axis=0)
-        first = jnp.concatenate(firsts, axis=0)
-        second = jnp.concatenate(seconds, axis=0)
-        mean = jnp.sum(40.0 * pivot + first, axis=1, keepdims=True) / 5120.0
-        gap = mean - pivot
-        spread = second - 2.0 * gap * first + 40.0 * gap * gap
-        scale = lax.rsqrt(jnp.sum(spread, axis=1, keepdims=True) / 5120.0 + 1e-06)
-        value = scale * (raw - mean * col_sum) + offset
-        for m in range(20):
-            row = (4 * n + m // 5) * 56 + 8 + (m % 5) * 8
-            grid[pl.ds(pl.multiple_of(row, 8), 8), :] = value[8 * m : 8 * m + 8]
+            moments[1, at] = second
+        raw[...] = jnp.dot(tokens[n], rhs[...], preferred_element_type=F32)
         return carry
 
     lax.fori_loop(0, 5, head_step, 0)
-
-    lane8 = lax.broadcasted_iota(jnp.int32, (8, 128), 1)
+    for k in range(2):
+        load_taps(k).start()
+    settle(4)
+
     for j in range(8):
         for pair in range(5):
             pieces = []
             for q in (2 * pair, 2 * pair + 1):
                 at = 56 * q + 7 + 5 * j
-                pieces.append(
-                    jnp.where(lane8 < 64, grid[at : at + 8, :], grid[560 + at : 568 + at, :])
-                )
+                pieces.append(grid[at : at + 8, :])
             outgoing[j, 16 * pair : 16 * pair + 16, :] = jnp.concatenate(pieces, axis=0).astype(
                 BF16
             )
 
-    pl.semaphore_wait(barrier, 3 * bands - 1)
-    copies = []
-    for o in range(bands):
+    def send(d, o):
         to = lax.rem(band + o, bands)
-        for d in range(3):
-            target = recv_ref.at[2 - d, band]
-            if d or o:
-                cp = pltpu.make_async_remote_copy(
-                    src_ref=outgoing.at[to],
-                    dst_ref=target,
-                    send_sem=send_sem.at[d, o],
-                    recv_sem=recv_sem.at[d, o],
-                    device_id=(lax.rem(slab + d, slabs), to),
-                    device_id_type=MESH,
-                )
-            else:
-                cp = pltpu.make_async_copy(outgoing.at[to], target, send_sem.at[d, o])
-            cp.start()
-            copies.append(cp)
+        return pltpu.make_async_remote_copy(
+            src_ref=outgoing.at[to],
+            dst_ref=recv_ref.at[2 - d, band],
+            send_sem=send_sem.at[d, o],
+            recv_sem=recv_sem.at[d, o],
+            device_id=(slab + d, to),
+            device_id_type=MESH,
+        )
+
+    pl.semaphore_wait(
+        barrier,
+        bands * jnp.minimum(slabs - slab, 3) - 1,
+    )
+    for d in (2, 1, 0):
+
+        @pl.when(slab + d < slabs)
+        def _():
+            for o in range(1, bands + 1):
+                if d or o < bands:
+                    send(d, o % bands).start()
+
+    own_copy = pltpu.make_async_copy(outgoing.at[band], recv_ref.at[2, band], small_sem.at[0])
+    own_copy.start()
 
     win_copy.wait()
     blank = jnp.zeros((16, 384), BF16)
@@ -414,34 +439,52 @@
                         dense_in[row : row + 16, col : col + 384] = (
                             win[9 * a + 3 * b + e] * half if ok else blank
                         )
-    dense_store = pltpu.make_async_copy(dense_in, dense_ref, store_sem.at[2])
+    dense_store = pltpu.make_async_copy(dense_in, dense_ref, store_sem.at[3])
     dense_store.start()
 
-    second = 2 * slab + 1
-    starts = second == 0
+    second_frame = 2 * slab + 1
+    starts = second_frame == 0
     end = jnp.int32(0)
     for clip in range(clip_ref.shape[0] - 1):
         end = end + clip_ref[clip]
-        starts = jnp.logical_or(starts, second == end)
-    for cp in raw_copies:
-        cp.wait()
+        starts = jnp.logical_or(starts, second_frame == end)
+
+    def store_mixed(k):
+        at = pl.ds(3 * k, 3)
+        return pltpu.make_async_copy(mixed.at[:, at], mixed_ref.at[:, at], store_sem.at[k])
 
     def mix(k, carry):
-        w0, w1, w2 = (raw[a, k].astype(F32) for a in range(3))
-        outer = 0.5 * (w0 + w2)
-        mid = 0.5 * w1
-        mixed[0, k] = jnp.where(starts, w1, outer + mid).astype(BF16)
-        mixed[1, k] = jnp.where(starts, w2, outer - mid).astype(BF16)
+        w0, w1, w2 = (taps[a, k].astype(F32) for a in range(3))
+        outer = w0 + w2
+        mixed[0, k] = jnp.where(starts, taps[1, k], (outer + w1).astype(BF16))
+        mixed[1, k] = jnp.where(starts, taps[2, k], (outer - w1).astype(BF16))
         return carry
 
-    lax.fori_loop(0, 9, mix, 0)
-    mixed_stores = [
-        pltpu.make_async_copy(mixed.at[i], mixed_ref.at[i], store_sem.at[i]) for i in range(2)
-    ]
-    for cp in mixed_stores:
-        cp.start()
-    for cp in copies + mixed_stores + [dense_store]:
-        cp.wait()
+    for k in range(3):
+        load_taps(k).wait()
+        if k == 0:
+            load_taps(2).start()
+        lax.fori_loop(3 * k, 3 * k + 3, mix, 0)
+        store_mixed(k).start()
+
+    own_copy.wait()
+    for d in range(3):
+
+        @pl.when(slab + d < slabs)
+        def _():
+            for o in range(bands):
+                if d or o:
+                    send(d, o).wait_send()
+
+        @pl.when(slab >= d)
+        def _():
+            for o in range(bands):
+                if d or o:
+                    send(d, o).wait_recv()
+
+    dense_store.wait()
+    for k in range(3):
+        store_mixed(k).wait()
 
 
 def head(
@@ -457,8 +500,8 @@
         in_specs=[
             pl.BlockSpec(memory_space=pltpu.SMEM),
             pl.BlockSpec(memory_space=pl.ANY),
-            pl.BlockSpec(memory_space=pltpu.VMEM),
-            pl.BlockSpec(memory_space=pltpu.VMEM),
+            pl.BlockSpec(memory_space=pl.ANY),
+            pl.BlockSpec(memory_space=pl.ANY),
             pl.BlockSpec(memory_space=pltpu.VMEM),
             pl.BlockSpec(memory_space=pl.ANY),
             pl.BlockSpec(memory_space=pl.ANY),
@@ -466,17 +509,22 @@
         out_specs=[pl.BlockSpec(memory_space=pl.ANY)] * 3,
         scratch_shapes=[
             pltpu.VMEM((5, 160, 5120), BF16),
-            pltpu.VMEM((256, 5120), BF16),
+            pltpu.VMEM((2, 4, 5120), F32),
+            pltpu.VMEM((64, 5120), BF16),
+            pltpu.VMEM((5120, 256), BF16),
             pltpu.VMEM((16, 5120), BF16),
-            pltpu.VMEM((1120, 128), F32),
+            pltpu.VMEM((160, 256), F32),
+            pltpu.VMEM((2, 160, 128), F32),
+            pltpu.VMEM((560, 128), F32),
             pltpu.VMEM((8, 80, 128), BF16),
             pltpu.VMEM((27, 16, 384), BF16),
             pltpu.VMEM((768, 1536), BF16),
             pltpu.VMEM((3, 9, 384, 384), BF16),
             pltpu.VMEM((2, 9, 384, 384), BF16),
             pltpu.SemaphoreType.DMA((5,)),
+            pltpu.SemaphoreType.DMA((3,)),
+            pltpu.SemaphoreType.DMA((3,)),
             pltpu.SemaphoreType.DMA((4,)),
-            pltpu.SemaphoreType.DMA((3,)),
             pltpu.SemaphoreType.DMA((3, 8)),
             pltpu.SemaphoreType.DMA((3, 8)),
         ],
@@ -490,7 +538,7 @@
         head_weight.T,
         head_bias,
         conv_in_weight.reshape(27, 16, 384),
-        conv_out_weight.reshape(27, 384, 384),
+        conv_out_weight.reshape(3, 9, 384, 384),
     )
 
 

time: 53.2 us -> 51.7 us (0.972)
  Pallas kernels: 52.9 us -> 51.4 us
    pallas_call x1, Pallas kernels: 21.6 us -> 20.2 us  [head(): pl.pallas_call(head_kernel, out_shape=(jax.ShapeDtypeStruct((3, 8, 80, 12...]
where the time goes in v2:
time: 51.7 us; the launch traced here: 51.5 us
  Pallas kernels  51.4 us (99%)
    pallas_call x1, Pallas kernels, convolve(): pl.pallas_call(functools.partial(conv_kernel, rows_per_step=R), out_shape...  31.2 us
    pallas_call x1, Pallas kernels, head(): pl.pallas_call(head_kernel, out_shape=(jax.ShapeDtypeStruct((3, 8, 80, 12...  20.2 us

profile of v2, /device:TPU:0, one launch (start us, length us, event | category | flops | bytes accessed | tf_op | source)
XLA Modules:
  0.0 51.5 jit_solution(11208002399353630619)
XLA Ops:
  0.0 20.2 %shard_map.91 = (bf16[3,8,80,128]{3,2,1,0:T(8,128)(2,1)}, bf16[768,1536]{1,0:T(8,128)(2,1)}, bf16[2,9,384,384]{3,2,1,0:T(8,128)(2,1)}) custom-call(s32[4]{0:T(128)} %clip_ref.3, bf16[800,5120]{1,0:T(8,128)(2,1)} %bitcast.9, f32[2,4,5120]{2,1,0:T(4,128)} %mod_ref.1, bf16[64,5120]{1,0:T(8,128)(2,1)} %bitcast.10, f32[64]{0:T(128)} %bias_ref.1, ...), custom_call_target="tpu_custom_call" | custom-call | tf_op jit(solution)/shard_map/pallas_call | solution.py:493
  20.2 31.2 %shard_map.92 = bf16[2,10,160,384]{3,2,1,0:T(8,128)(2,1)} custom-call(s32[4]{0:T(128)} %clip_ref.3, bf16[3,8,80,128]{3,2,1,0:T(8,128)(2,1)} %get-tuple-element.8.recv_ref, bf16[768,1536]{1,0:T(8,128)(2,1)} %get-tuple-element.9.dense_ref, f32[384]{0:T(512)} %bin_ref.1, bf16[27,384,384]{2,1,0:T(8,128)(2,1)} %bitcast.8, ...), custom_call_target="tpu_custom_call" | custom-call | tf_op jit(solution)/shard_map/pallas_call | solution.py:239

commit v3 on v2

--- a/solution.py
+++ b/solution.py
@@ -89,15 +89,15 @@
     for i in (1, 2, 0, 3):
         loads[i].start()
 
-    def in_step(step, carry):
+    def in_step(step):
         i0 = 2 * step
         for p in range(2):
             x = []
             for g in range(4):
                 parts = []
                 for a in range(3):
-                    lo = tokens[g + a, pl.ds(pl.multiple_of(i0 * 80, 16), 160), :]
-                    hi = tokens[g + a, pl.ds(pl.multiple_of(i0 * 80 + 80, 16), 160), :]
+                    lo = tokens[g + a, pl.ds(i0 * 80, 160), :]
+                    hi = tokens[g + a, pl.ds(i0 * 80 + 80, 160), :]
                     both = jnp.concatenate([lo, hi], axis=1)
                     if a < 2:
                         both = jnp.where(keep[g][a], both, jnp.zeros_like(both))
@@ -118,9 +118,9 @@
             for r in range(2):
                 for i in range(4):
                     inner[i, 4 * step + 2 * r + p] = sums[i][80 * r : 80 * r + 80]
-        return carry
-
-    lax.fori_loop(0, 3, in_step, 0)
+
+    for step in range(3):
+        in_step(step)
 
     @pl.when(band == 0)
     def _():
@@ -200,40 +200,36 @@
 
     at = (0, 768, 1152, 1536)
 
-    def finish_both(h0):
-        for f in range(2):
-            finish(f, h0, *[total[f, :, at[n] : at[n + 1]] for n in range(3)])
-
-    def out_step(step, carry):
-        h0 = step * R
-        finish_both(jnp.maximum(h0 - R, 0))
+    def finish_one(f, h0):
+        finish(f, h0, *[total[f, :, at[n] : at[n + 1]] for n in range(3)])
+
+    for h0 in range(0, 10, R):
+        if h0 > 0:
+            for f in range(2):
+                finish_one(f, h0 - R)
         m1 = product(1, h0)
         m2 = product(2, h0)
         m0 = product(0, h0)
         for n, (u, v, w) in enumerate(zip(m0, m1, m2)):
             total[0, :, at[n] : at[n + 1]] = u + halved * (v + w)
             total[1, :, at[n] : at[n + 1]] = paired * (v - w)
+        if h0 + R == 10:
+            finish_one(0, h0)
         for n, u in enumerate(product(3, h0)):
             total[1, :, at[n] : at[n + 1]] = total[1, :, at[n] : at[n + 1]] + u
-
-        @pl.when(step > 0)
-        def _():
-            store(0, h0 - R).start()
-            store(1, h0 - R).start()
-
-        return carry
-
-    lax.fori_loop(0, 10 // R, out_step, 0)
-    finish_both(10 - R)
-    for f in range(2):
-        store(f, 10 - R).start()
+        if h0 > 0:
+            for f in range(2):
+                store(f, h0 - R).start()
+    store(0, 10 - R).start()
+    finish_one(1, 10 - R)
+    store(1, 10 - R).start()
     for f in range(2):
         pltpu.make_async_copy(packed.at[f], out_ref.at[f], store_sem.at[f]).wait()
 
 
 def convolve(
     clip_lengths, received, dense_in, conv_in_bias, conv_out_weight, mixed, conv_out_bias,
-    rows_per_step=5,
+    rows_per_step=2,
 ):
     R = rows_per_step
     return pl.pallas_call(

time: 51.7 us -> 49.6 us (0.959)
  Pallas kernels: 51.4 us -> 49.2 us
    pallas_call x1, Pallas kernels: 31.2 us -> 29.1 us  [convolve(): pl.pallas_call(functools.partial(conv_kernel, rows_per_step=R), out_shape...]
where the time goes in v3:
time: 49.6 us; the launch traced here: 49.4 us
  Pallas kernels  49.2 us (99%)
    pallas_call x1, Pallas kernels, convolve(): pl.pallas_call(functools.partial(conv_kernel, rows_per_step=R), out_shape...  29.1 us
    pallas_call x1, Pallas kernels, head(): pl.pallas_call(head_kernel, out_shape=(jax.ShapeDtypeStruct((3, 8, 80, 12...  20.2 us

profile of v3, /device:TPU:0, one launch (start us, length us, event | category | flops | bytes accessed | tf_op | source)
XLA Modules:
  0.0 49.4 jit_solution(787605109645701112)
XLA Ops:
  0.0 20.2 %shard_map.91 = (bf16[3,8,80,128]{3,2,1,0:T(8,128)(2,1)}, bf16[768,1536]{1,0:T(8,128)(2,1)}, bf16[2,9,384,384]{3,2,1,0:T(8,128)(2,1)}) custom-call(s32[4]{0:T(128)} %clip_ref.3, bf16[800,5120]{1,0:T(8,128)(2,1)} %bitcast.9, f32[2,4,5120]{2,1,0:T(4,128)} %mod_ref.1, bf16[64,5120]{1,0:T(8,128)(2,1)} %bitcast.10, f32[64]{0:T(128)} %bias_ref.1, ...), custom_call_target="tpu_custom_call" | custom-call | tf_op jit(solution)/shard_map/pallas_call | solution.py:489
  20.2 29.1 %shard_map.92 = bf16[2,10,160,384]{3,2,1,0:T(8,128)(2,1)} custom-call(s32[4]{0:T(128)} %clip_ref.3, bf16[3,8,80,128]{3,2,1,0:T(8,128)(2,1)} %get-tuple-element.8.recv_ref, bf16[768,1536]{1,0:T(8,128)(2,1)} %get-tuple-element.9.dense_ref, f32[384]{0:T(512)} %bin_ref.1, bf16[27,384,384]{2,1,0:T(8,128)(2,1)} %bitcast.8, ...), custom_call_target="tpu_custom_call" | custom-call | tf_op jit(solution)/shard_map/pallas_call | solution.py:235

commit v4 on v3

--- a/solution.py
+++ b/solution.py
@@ -22,8 +22,8 @@
 
 
 def conv_kernel(
-    clip_ref, recv_ref, dense_ref, bin_ref, wout_ref, mixed_ref, bout_ref, out_ref,
-    received, spread, tokens, dense_in, inner, weights, total, stage, packed,
+    clip_ref, recv_ref, win_ref, bin_ref, wout_ref, mixed_ref, bout_ref, out_ref,
+    received, win, spread, tokens, dense_in, inner, weights, total, stage, packed,
     recv_sem, load_sem, store_sem, *, rows_per_step,
 ):
     slab = lax.axis_index("tm")
@@ -31,9 +31,9 @@
     frame0 = 2 * slab
 
     recv_copy = pltpu.make_async_copy(recv_ref, received, recv_sem)
+    win_copy = pltpu.make_async_copy(win_ref, win, load_sem.at[4])
+    win_copy.start()
     recv_copy.start()
-    dense_copy = pltpu.make_async_copy(dense_ref, dense_in, load_sem.at[4])
-    dense_copy.start()
     sources = (
         wout_ref.at[pl.ds(0, 9)], mixed_ref.at[0], mixed_ref.at[1], wout_ref.at[pl.ds(18, 9)]
     )
@@ -41,6 +41,21 @@
         pltpu.make_async_copy(sources[i], weights.at[i], load_sem.at[i]) for i in range(4)
     ]
 
+    win_copy.wait()
+    blank = jnp.zeros((16, 384), BF16)
+    half = jnp.asarray(0.5, BF16)
+    for a in range(3):
+        for rr in range(4):
+            for slot in range(4):
+                for p in range(2):
+                    for s in range(2):
+                        b, e = rr - p, slot - s
+                        ok = 0 <= b < 3 and 0 <= e < 3
+                        row = a * 256 + rr * 64 + slot * 16
+                        col = (2 * p + s) * 384
+                        dense_in[row : row + 16, col : col + 384] = (
+                            win[9 * a + 3 * b + e] * half if ok else blank
+                        )
     lane_in = lax.broadcasted_iota(jnp.int32, (128, 256), 0)
     lane_out = lax.broadcasted_iota(jnp.int32, (128, 256), 1)
     wanted = (
@@ -53,6 +68,8 @@
     slot_id = (lax.broadcasted_iota(jnp.int32, (7, 10, 8, 128), 3) // 16) % 4
     group_id = lax.broadcasted_iota(jnp.int32, (7, 1, 8, 128), 2)
     recv_copy.wait()
+    for i in (1, 2, 0, 3):
+        loads[i].start()
     for back in range(3):
         for src in range(8):
             block = received[back, src].astype(F32)
@@ -85,9 +102,6 @@
     paired = jnp.where(joined, 0.5, 0.0).astype(F32)
     bias_in = 0.5 * bin_ref[...].reshape(1, 384)
     bias_in = jnp.concatenate([bias_in, bias_in], axis=1)
-    dense_copy.wait()
-    for i in (1, 2, 0, 3):
-        loads[i].start()
 
     def in_step(step):
         i0 = 2 * step
@@ -228,7 +242,7 @@
 
 
 def convolve(
-    clip_lengths, received, dense_in, conv_in_bias, conv_out_weight, mixed, conv_out_bias,
+    clip_lengths, received, conv_in_weight, conv_in_bias, conv_out_weight, mixed, conv_out_bias,
     rows_per_step=2,
 ):
     R = rows_per_step
@@ -247,6 +261,7 @@
         out_specs=pl.BlockSpec(memory_space=pl.ANY),
         scratch_shapes=[
             pltpu.VMEM((3, 8, 80, 128), BF16),
+            pltpu.VMEM((27, 16, 384), BF16),
             pltpu.VMEM((3, 640, 128), F32),
             pltpu.VMEM((6, 560, 128), BF16),
             pltpu.VMEM((768, 1536), BF16),
@@ -261,15 +276,14 @@
         ],
         compiler_params=pltpu.CompilerParams(vmem_limit_bytes=60 << 20),
     )(
-        clip_lengths, received, dense_in, conv_in_bias,
+        clip_lengths, received, conv_in_weight.reshape(27, 16, 384), conv_in_bias,
         conv_out_weight.reshape(27, 384, 384), mixed, conv_out_bias,
     )
 
 
 def head_kernel(
-    clip_ref, hidden_ref, mod_ref, weight_ref, bias_ref, win_ref, wout_ref,
-    recv_ref, dense_ref, mixed_ref,
-    tokens, mod, weight, rhs, aux, raw, moments, grid, outgoing, win, dense_in, taps, mixed,
+    clip_ref, hidden_ref, mod_ref, weight_ref, bias_ref, wout_ref, recv_ref, mixed_ref,
+    tokens, mod, weight, rhs, aux, raw, moments, grid, outgoing, taps, mixed,
     load_sem, small_sem, tap_sem, store_sem, send_sem, recv_sem,
 ):
     slab = lax.axis_index("tm")
@@ -290,8 +304,6 @@
 
     for n in range(1):
         load(n).start()
-    win_copy = pltpu.make_async_copy(win_ref, win, small_sem.at[2])
-    win_copy.start()
 
     barrier = pltpu.get_barrier_semaphore()
     for d in range(3):
@@ -380,8 +392,6 @@
         return carry
 
     lax.fori_loop(0, 5, head_step, 0)
-    for k in range(2):
-        load_taps(k).start()
     settle(4)
 
     for j in range(8):
@@ -413,30 +423,15 @@
 
         @pl.when(slab + d < slabs)
         def _():
-            for o in range(1, bands + 1):
-                if d or o < bands:
-                    send(d, o % bands).start()
+            for o in (4, 5, 3, 6, 2, 7, 1, 0):
+                if d or o:
+                    send(d, o).start()
 
     own_copy = pltpu.make_async_copy(outgoing.at[band], recv_ref.at[2, band], small_sem.at[0])
     own_copy.start()
 
-    win_copy.wait()
-    blank = jnp.zeros((16, 384), BF16)
-    half = jnp.asarray(0.5, BF16)
-    for a in range(3):
-        for rr in range(4):
-            for slot in range(4):
-                for p in range(2):
-                    for s in range(2):
-                        b, e = rr - p, slot - s
-                        ok = 0 <= b < 3 and 0 <= e < 3
-                        row = a * 256 + rr * 64 + slot * 16
-                        col = (2 * p + s) * 384
-                        dense_in[row : row + 16, col : col + 384] = (
-                            win[9 * a + 3 * b + e] * half if ok else blank
-                        )
-    dense_store = pltpu.make_async_copy(dense_in, dense_ref, store_sem.at[3])
-    dense_store.start()
+    for k in range(2):
+        load_taps(k).start()
 
     second_frame = 2 * slab + 1
     starts = second_frame == 0
@@ -478,19 +473,17 @@
                 if d or o:
                     send(d, o).wait_recv()
 
-    dense_store.wait()
     for k in range(3):
         store_mixed(k).wait()
 
 
 def head(
-    clip_lengths, hidden, modulation, head_weight, head_bias, conv_in_weight, conv_out_weight
+    clip_lengths, hidden, modulation, head_weight, head_bias, conv_out_weight
 ):
     return pl.pallas_call(
         head_kernel,
         out_shape=(
             jax.ShapeDtypeStruct((3, 8, 80, 128), BF16),
-            jax.ShapeDtypeStruct((768, 1536), BF16),
             jax.ShapeDtypeStruct((2, 9, 384, 384), BF16),
         ),
         in_specs=[
@@ -500,9 +493,8 @@
             pl.BlockSpec(memory_space=pl.ANY),
             pl.BlockSpec(memory_space=pltpu.VMEM),
             pl.BlockSpec(memory_space=pl.ANY),
-            pl.BlockSpec(memory_space=pl.ANY),
         ],
-        out_specs=[pl.BlockSpec(memory_space=pl.ANY)] * 3,
+        out_specs=[pl.BlockSpec(memory_space=pl.ANY)] * 2,
         scratch_shapes=[
             pltpu.VMEM((5, 160, 5120), BF16),
             pltpu.VMEM((2, 4, 5120), F32),
@@ -513,8 +505,6 @@
             pltpu.VMEM((2, 160, 128), F32),
             pltpu.VMEM((560, 128), F32),
             pltpu.VMEM((8, 80, 128), BF16),
-            pltpu.VMEM((27, 16, 384), BF16),
-            pltpu.VMEM((768, 1536), BF16),
             pltpu.VMEM((3, 9, 384, 384), BF16),
             pltpu.VMEM((2, 9, 384, 384), BF16),
             pltpu.SemaphoreType.DMA((5,)),
@@ -533,7 +523,6 @@
         modulation,
         head_weight.T,
         head_bias,
-        conv_in_weight.reshape(27, 16, 384),
         conv_out_weight.reshape(3, 9, 384, 384),
     )
 
@@ -542,11 +531,11 @@
     hidden, modulation, clip_lengths, head_weight, head_bias,
     conv_in_weight, conv_in_bias, conv_out_weight, conv_out_bias,
 ):
-    received, dense_in, mixed = head(
-        clip_lengths, hidden, modulation, head_weight, head_bias, conv_in_weight, conv_out_weight
+    received, mixed = head(
+        clip_lengths, hidden, modulation, head_weight, head_bias, conv_out_weight
     )
     return convolve(
-        clip_lengths, received, dense_in, conv_in_bias, conv_out_weight, mixed, conv_out_bias
+        clip_lengths, received, conv_in_weight, conv_in_bias, conv_out_weight, mixed, conv_out_bias
     )
 
 

time: 49.6 us -> 49.6 us (level)
  no operation moved by 1% of the time
where the time goes in v4:
time: 49.6 us; the launch traced here: 49.4 us
  Pallas kernels  49.3 us (99%)
    pallas_call x1, Pallas kernels, convolve(): pl.pallas_call(functools.partial(conv_kernel, rows_per_step=R), out_shape...  28.9 us
    pallas_call x1, Pallas kernels, head(): pl.pallas_call(head_kernel, out_shape=(jax.ShapeDtypeStruct((3, 8, 80, 12...  20.4 us

profile of v4, /device:TPU:0, one launch (start us, length us, event | category | flops | bytes accessed | tf_op | source)
XLA Modules:
  0.0 49.4 jit_solution(4146739249800584548)
XLA Ops:
  0.0 20.4 %shard_map.91 = (bf16[3,8,80,128]{3,2,1,0:T(8,128)(2,1)}, bf16[2,9,384,384]{3,2,1,0:T(8,128)(2,1)}) custom-call(s32[4]{0:T(128)} %clip_ref.3, bf16[800,5120]{1,0:T(8,128)(2,1)} %bitcast.9, f32[2,4,5120]{2,1,0:T(4,128)} %mod_ref.1, bf16[64,5120]{1,0:T(8,128)(2,1)} %bitcast.10, f32[64]{0:T(128)} %bias_ref.1, bf16[3,9,384,384]{3,2,1,0:T(8,128)(2,1)} %bitcast.7), custom_call_target="tpu_custom_call" | custom-call | tf_op jit(solution)/shard_map/pallas_call | solution.py:483
  20.4 28.9 %shard_map.92 = bf16[2,10,160,384]{3,2,1,0:T(8,128)(2,1)} custom-call(s32[4]{0:T(128)} %clip_ref.3, bf16[3,8,80,128]{3,2,1,0:T(8,128)(2,1)} %get-tuple-element.7.recv_ref, bf16[27,16,384]{2,1,0:T(8,128)(2,1)} %bitcast.11, f32[384]{0:T(512)} %bin_ref.1, bf16[27,384,384]{2,1,0:T(8,128)(2,1)} %bitcast.8, bf16[2,9,384,384]{3,2,1,0:T(8,128)(2,1)} %get-tuple-element.8.mixed_ref, ...), custom_call_target="tpu_custom_call" | custom-call | tf_op jit(solution)/shard_map/pallas_call | solution.py:249
